TPU v7x, 32 devices: a whole 2x2x4 slice. The times are simulated.
32 devices in a mesh: expert: 2 (over x), row: 4 (over z), col: 4 (over y, core).
Axes of the slice: x: 2, y: 2, z: 4, core: 2. Of those that a mesh axis runs over, the one named last changes fastest.
Arguments:
- tokens: bfloat16 [2048, 3584], P(('expert', 'col'), 'row'), may hold values from -6 to 6
- slots: int32 [8, 6, 2, 2], P(('expert', 'col')), may hold values from 0 to 255
- counts: int32 [6, 2], replicated, may hold values from 1 to 16, as said below
- owner: int32 [2], replicated, may hold values from 0 to 1, each once
Outputs:
- moments: float32 [2, 3584, 3584], P('expert', 'row', 'col')
Inputs may be any that keep to these rules, and one draw needn't show every extreme that they name: `counts`: in every panel at least one expert's count is 16.
All inputs are finite; a program needn't handle non-finite values.
Results may differ from a plain program's by a relative error of at most 0.0003.
Values may be sent and summed in bfloat16 or wider, within the bound.
A program may use at most 64 MiB of HBM per device.

v0:
```python
import jax
import jax.numpy as jnp
from jax import lax
from jax.sharding import PartitionSpec as P


def from_root(value, axis, root):
    mine = lax.axis_index(axis) == root
    return lax.psum(jnp.where(mine, value, jnp.zeros_like(value)), axis)


def panel_moment(outgoing):
    received = lax.all_to_all(outgoing, "expert", split_axis=1, concat_axis=1, tiled=True)
    panel_count = received.shape[0]
    feature_count = received.shape[3]
    left_rows = lax.all_gather(received, "col", axis=2, tiled=True)
    left_rows = left_rows.reshape(panel_count, -1, feature_count)
    right_rows = from_root(left_rows, "row", lax.axis_index("col"))
    return jnp.einsum("kpa,kpb->ab", left_rows, right_rows, preferred_element_type=jnp.float32)


def per_device(tokens, slots, counts, owner):
    col_count = lax.axis_size("col")
    slot_count = slots.shape[3]
    block_index = lax.axis_index("expert") * col_count + lax.axis_index("col")
    inverse = jnp.argsort(owner)
    dest_slots = jnp.take(slots[0], inverse, axis=1)
    dest_counts = jnp.take(counts, inverse, axis=1)
    position = block_index * slot_count + jnp.arange(slot_count, dtype=jnp.int32)
    usable = position[None, None, :] < dest_counts[:, :, None]
    picked = tokens[dest_slots]
    outgoing = jnp.where(usable[..., None], picked, jnp.zeros_like(picked))
    own_expert = inverse[lax.axis_index("expert")]
    row_total = jnp.sum(jnp.take(counts, own_expert, axis=1)).astype(jnp.float32)
    moment_tile = panel_moment(outgoing)
    return (moment_tile / row_total)[None]


def solution(mesh):
    return jax.shard_map(
        per_device,
        mesh=mesh,
        in_specs=(P(("expert", "col"), "row"), P(("expert", "col"), None, None, None), P(), P()),
        out_specs=P("expert", "row", "col"),
        check_vma=False,
    )
```

profile of v0, /device:TPU:0, one launch (start us, length us, event | category | flops | bytes accessed | tf_op | source)
XLA Modules:
  0.0 72.3 jit_solution(10034563110753192269)
XLA Ops:
  6.5 0.0 copy-start
  6.5 1.3 %sort.17 = (s32[2]{0:T(128)}, s32[2]{0:T(128)S(1)}) sort(s32[2]{0:T(128)} %param.7, s32[2]{0:T(128)S(1)} %iota.10), dimensions={0}, to_apply=%region_0.0 | sort | flops 2 | bytes 32 | tf_op jit(solution)/shard_map/jit(argsort)/sort | solution.py:26
  7.9 1.2 %gather_fusion = s32[2,6]{1,0:T(2,128)S(1)} fusion(s32[6,2]{0,1:T(2,128)} %param.6, s32[1024]{0:T(1024)S(1)} %pad_clamp_fusion.1), kind=kCustom, calls=%fused_computation | custom fusion | bytes 104 | tf_op jit(solution)/shard_map/jit(_take)/gather | solution.py:28
  9.1 1.3 %gather_fusion.1 = s32[2,6,2]{1,2,0:T(2,128)S(1)} fusion(s32[6,2,2]{0,2,1:T(2,128)} %bitcast.23, s32[1024]{0:T(1024)S(1)} %pad_clamp_fusion.1), kind=kCustom, calls=%fused_computation.1 | custom fusion | bytes 200 | tf_op jit(solution)/shard_map/jit(_take)/gather | solution.py:27
  10.4 0.1 compare_select_fusion
  10.5 0.1 select_bitcast_fusion
  10.5 0.1 copy.9
  10.6 0.1 reshape.96
  10.7 0.0 copy-done
  10.8 0.6 gather_fusion.2
  11.4 0.1 broadcast_compare_fusion
  11.5 0.7 %broadcast_select_fusion = bf16[6,2,2,896]{3,2,0,1:T(2,128)(2,1)} fusion(pred[6,2,2]{2,0,1:T(8,128)(4,1)S(1)} %broadcast_compare_fusion, bf16[6,2,2,896]{3,2,1,0:T(2,128)(2,1)S(1)} %reshape.95), kind=kLoop, calls=%fused_computation.8 | loop fusion | flops 21504 | bytes 86040 | tf_op jit(solution)/shard_map/jit(_where)/select_n | solution.py:32
  12.2 4.2 %all-to-all-start = ((bf16[6,2,2,896]{3,2,0,1:T(2,128)(2,1)}), bf16[6,2,2,896]{3,2,0,1:T(2,128)(2,1)S(1)}, u32[]{:S(2)}, u32[]{:S(2)}) async-start(bf16[6,2,2,896]{3,2,0,1:T(2,128)(2,1)} %broadcast_select_fusion), calls=%async_computation | async-start | bytes 86016 | tf_op jit(solution)/shard_map/all_to_all | solution.py:13
  16.4 0.0 all-reduce.2.cloned.1.call-start
  16.4 4.0 %all-to-all-done = bf16[6,2,2,896]{3,2,0,1:T(2,128)(2,1)S(1)} async-done(((bf16[6,2,2,896]{3,2,0,1:T(2,128)(2,1)}), bf16[6,2,2,896]{3,2,0,1:T(2,128)(2,1)S(1)}, u32[]{:S(2)}, u32[]{:S(2)}) %all-to-all-start) | async-done | bytes 43040 | tf_op jit(solution)/shard_map/all_to_all | solution.py:13
  20.4 5.8 %all_gather.3 = bf16[6,2,8,896]{3,1,0,2:T(2,128)(2,1)S(1)} all-gather(bf16[6,2,2,896]{3,1,0,2:T(2,128)(2,1)S(1)} %copy.11), channel_id=1, replica_groups=mesh['expert'=2,'row'=4,'col'=4] {'col'}, dimensions={2}, use_global_device_ids=true | all-gather | bytes 215040 | tf_op jit(solution)/shard_map/all_gather | solution.py:16
  26.2 0.7 bitcast_select_fusion
  26.9 0.0 all-reduce.2.cloned.1.call-update
  27.0 0.6 dynamic_slice.3
  29.5 1.3 %fusion.3 = s32[]{:T(128)} fusion(pred[]{:T(512)S(6)} %and.16, s32[6,2]{0,1:T(2,128)} %param.6, s32[]{:T(128)S(6)} %select_n.68), kind=kLoop, calls=%fused_computation.18 | loop fusion | flops 11 | bytes 33 | tf_op jit(solution)/shard_map/reduce_sum | solution.py:34
  31.5 30.7 %all-reduce.2.cloned.1.call-done = bf16[6,16,896]{2,1,0:T(8,128)(2,1)} async-done(((bf16[6,16,896]{2,1,0:T(8,128)(2,1)}), bf16[6,16,896]{2,1,0:T(8,128)(2,1)}) %all-reduce.2.cloned.1.call-update) | async-done | bytes 172048 | tf_op jit(solution)/shard_map/psum | solution.py:9
  62.2 3.2 %fusion = f32[1,896,896]{2,1,0:T(8,128)} fusion(bf16[6,16,896]{2,1,0:T(8,128)(2,1)} %all-reduce.2.cloned.1.call-done, f32[]{:T(128)S(6)} %convert_element_type.3, bf16[6,2,8,896]{3,1,0,2:T(2,128)(2,1)S(1)} %all_gather.3), kind=kOutput, calls=%fused_computation.4 | convolution fusion | flops 154943488 | bytes 3555332 | tf_op jit(solution)/shard_map/kpa,kpb->ab/dot_general | solution.py:19
  (8 shorter events, 0.1 us)
Async XLA Ops:
  6.5 4.2 %copy-start = (bf16[256,896]{1,0:T(8,128)(2,1)S(1)}, bf16[256,896]{1,0:T(8,128)(2,1)}, u32[]{:S(2)}) copy-start(bf16[256,896]{1,0:T(8,128)(2,1)} %param.4) | copy-start | bytes 1376260
  12.2 8.2 %all-to-all-start = ((bf16[6,2,2,896]{3,2,0,1:T(2,128)(2,1)}), bf16[6,2,2,896]{3,2,0,1:T(2,128)(2,1)S(1)}, u32[]{:S(2)}, u32[]{:S(2)}) async-start(bf16[6,2,2,896]{3,2,0,1:T(2,128)(2,1)} %broadcast_select_fusion), calls=%async_computation | async-start | bytes 86016 | tf_op jit(solution)/shard_map/all_to_all | solution.py:13
  16.4 45.8 %all-reduce.2.cloned.1.call-start = ((), (), s32[]{:S(2)}) async-start(), calls=%async_computation.1 | async-start | bytes 344064 | tf_op jit(solution)/shard_map/psum | solution.py:9
Sparse Core Ops, SparseCore 0:
  27.1 35.0 all-reduce.1
where the time goes:
time: 72.6 us; the launch traced here: 72.3 us
  waiting for transfers between devices  34.7 us (48%)
  between operations  16 us (22%)
  blocking collectives  5.79 us (8%)
  other arithmetic  4.34 us (6%)
  starting transfers between devices  4.21 us (6%)
  local copies, waits for them, and re-layouts  3.98 us (5%)
  matrix products  3.22 us (4%)
    psum x1, waiting for transfers between devices, from_root(): return lax.psum(jnp.where(mine, value, jnp.zeros_like(value)), axis)  30.7 us
    all_gather x1, blocking collectives, panel_moment(): left_rows = lax.all_gather(received, 'col', axis=2, tiled=True)  5.79 us
    all_to_all x1, starting transfers between devices, panel_moment(): lax.all_to_all(outgoing, 'expert', split_axis=1, concat_axis=1, tiled=True)  4.21 us
    all_to_all x1, waiting for transfers between devices, panel_moment(): lax.all_to_all(outgoing, 'expert', split_axis=1, concat_axis=1, tiled=True)  4 us
    dot_general x1, matrix products, panel_moment(): jnp.einsum('kpa,kpb->ab', left_rows, right_rows, preferred_element_type=j...  3.22 us
  transfers between devices with their start and end apart: 2, of which 2 were waited for; matrix products, arithmetic and copies ran while one was open for 3% of the time, Pallas kernels for 0%

commit v1 on v0

v1 whole, which is shorter than its diff:
```python
import functools

import jax
import jax.numpy as jnp
from jax import lax
from jax.experimental import pallas as pl
from jax.experimental.pallas import tpu as pltpu
from jax.sharding import PartitionSpec as P

MESH = pl.DeviceIdType.MESH


def each(count, body):
    if count <= 4:
        for i in range(count):
            body(i)
    else:
        pl.loop(0, count)(body)


def wrap(index, count):
    return lax.rem(index + count, count)


def expert_of(owner_ref, group, expert_count):
    found = jnp.int32(0)
    for e in range(expert_count):
        found = jnp.where(owner_ref[e] == group, jnp.int32(e), found)
    return found


def exchange(sizes, owner_ref, counts_ref, slots_ref, tokens_ref, buf, tokens, picked, token_sem, own_sem, send_sem, recv_sem):
    n_group, n_row, n_col = sizes
    block_tokens, features = tokens_ref.shape
    panels, experts = counts_ref.shape
    slot_count = slots_ref.shape[3]
    padded = picked.shape[1]
    x, r, c = lax.axis_index("expert"), lax.axis_index("row"), lax.axis_index("col")
    block = x * n_col + c

    load = pltpu.make_async_copy(tokens_ref, tokens, token_sem)
    load.start()

    barrier = pltpu.get_barrier_semaphore()

    def greet(row, first_group, first_col):
        def per_group(dg):
            group = wrap(x + dg, n_group)
            for dc in range(n_col):
                def signal(group=group, dc=dc):
                    pl.semaphore_signal(
                        barrier, inc=1, device_id=(group, row, wrap(c + dc, n_col)), device_id_type=MESH
                    )
                if first_col and dc == 0:
                    pl.when(group != x)(signal)
                else:
                    signal()
        each(n_group, per_group)

    greet(r, 0, True)

    @pl.when(r != c)
    def _():
        greet(c, 0, False)

    load.wait()
    rows_iota = lax.broadcasted_iota(jnp.int32, (padded, block_tokens), 0)
    token_iota = lax.broadcasted_iota(jnp.int32, (padded, block_tokens), 1)

    def pick(dg):
        group = wrap(x + dg, n_group)
        e = expert_of(owner_ref, group, experts)
        index = jnp.full((padded, block_tokens), -1, jnp.int32)
        for k in range(panels):
            count = counts_ref[k, e]
            for j in range(slot_count):
                slot = jnp.where(block * slot_count + j < count, slots_ref[0, k, e, j], jnp.int32(-1))
                index = jnp.where(rows_iota == k * slot_count + j, slot, index)
        onehot = (index == token_iota).astype(jnp.bfloat16)
        picked[group] = jnp.dot(onehot, tokens[...], preferred_element_type=jnp.float32).astype(jnp.bfloat16)

    each(n_group, pick)
    pl.semaphore_wait(barrier, n_group * (n_row - 1) + n_group * n_col - 1)

    own = pltpu.make_async_copy(picked.at[x], buf.at[0, block], own_sem)

    def right_copy(dg, dr):
        group = wrap(x + dg, n_group)
        return pltpu.make_async_remote_copy(
            src_ref=picked.at[group],
            dst_ref=buf.at[1, block],
            send_sem=send_sem.at[1, dg, dr],
            recv_sem=recv_sem.at[1, block],
            device_id=(group, wrap(r + dr, n_row), r),
            device_id_type=MESH,
        )

    def left_copy(dg, dc):
        group = wrap(x + dg, n_group)
        return pltpu.make_async_remote_copy(
            src_ref=picked.at[group],
            dst_ref=buf.at[0, block],
            send_sem=send_sem.at[0, dg, dc],
            recv_sem=recv_sem.at[0, block],
            device_id=(group, r, wrap(c + dc, n_col)),
            device_id_type=MESH,
        )

    def all_copies(act):
        def right(dg):
            for dr in range(1, n_row):
                act(right_copy(dg, dr))

        def left(dg):
            for dc in range(n_col):
                if dc > 0:
                    act(left_copy(dg, dc))
                elif isinstance(dg, int):
                    if dg > 0:
                        act(left_copy(dg, dc))
                else:
                    pl.when(dg > 0)(lambda: act(left_copy(dg, 0)))

        each(n_group, right)
        each(n_group, left)

    all_copies(lambda copy: copy.start())
    own.start()

    def arrived(side, b):
        pltpu.make_async_remote_copy(
            src_ref=picked.at[0],
            dst_ref=buf.at[side, b],
            send_sem=send_sem.at[0, 0, 0],
            recv_sem=recv_sem.at[side, b],
            device_id=(x, r, c),
            device_id_type=MESH,
        ).wait_recv()

    def wait_left(dg):
        for dc in range(n_col):
            b = wrap(x + dg, n_group) * n_col + wrap(c + dc, n_col)
            if dc > 0:
                arrived(0, b)
            elif isinstance(dg, int):
                if dg > 0:
                    arrived(0, b)
            else:
                pl.when(dg > 0)(lambda: arrived(0, b))

    def wait_right(dg):
        for dc in range(n_col):
            arrived(1, wrap(x + dg, n_group) * n_col + dc)

    own.wait()
    all_copies(lambda copy: copy.wait_send())
    each(n_group, wait_left)

    @pl.when(r != c)
    def _():
        each(n_group, wait_right)


def multiply(tile, owner_ref, counts_ref, rows_ref, out_ref, product, sems):
    panels, experts = counts_ref.shape
    features = rows_ref.shape[-1]
    x, r, c = lax.axis_index("expert"), lax.axis_index("row"), lax.axis_index("col")
    e = expert_of(owner_ref, x, experts)
    total = jnp.int32(0)
    for k in range(panels):
        total = total + counts_ref[k, e]
    scale = 1.0 / jnp.full((1, features), total, jnp.int32).astype(jnp.float32)
    side = jnp.where(r == c, 0, 1)
    right = rows_ref[side].reshape(-1, features)
    copies = []
    for t in range(features // tile):
        span = pl.ds(t * tile, tile)
        left = rows_ref[0, :, :, span].reshape(-1, tile)
        part = lax.dot_general(left, right, (((0,), (0,)), ((), ())), preferred_element_type=jnp.float32)
        product[span, :] = part * scale
        copy = pltpu.make_async_copy(product.at[span, :], out_ref.at[0, span, :], sems.at[t])
        copy.start()
        copies.append(copy)
    for copy in copies:
        copy.wait()


def per_device(tokens, slots, counts, owner):
    n_group, n_row, n_col = lax.axis_size("expert"), lax.axis_size("row"), lax.axis_size("col")
    block_tokens, features = tokens.shape
    panels, slot_count = counts.shape[0], slots.shape[3]
    padded = -(-panels * slot_count // 16) * 16
    blocks = n_group * n_col
    smem = pl.BlockSpec(memory_space=pltpu.SMEM)
    rows = pl.pallas_call(
        functools.partial(exchange, (n_group, n_row, n_col)),
        out_shape=jax.ShapeDtypeStruct((2, blocks, padded, features), tokens.dtype),
        in_specs=[smem, smem, smem, pl.BlockSpec(memory_space=pl.ANY)],
        out_specs=pl.BlockSpec(memory_space=pltpu.VMEM),
        scratch_shapes=[
            pltpu.VMEM((block_tokens, features), tokens.dtype),
            pltpu.VMEM((n_group, padded, features), tokens.dtype),
            pltpu.SemaphoreType.DMA,
            pltpu.SemaphoreType.DMA,
            pltpu.SemaphoreType.DMA((2, n_group, max(n_row, n_col))),
            pltpu.SemaphoreType.DMA((2, blocks)),
        ],
        compiler_params=pltpu.CompilerParams(
            collective_id=0, has_side_effects=True, vmem_limit_bytes=32 * 1024 * 1024
        ),
    )(owner, counts, slots, tokens)
    tile = 128
    return pl.pallas_call(
        functools.partial(multiply, tile),
        out_shape=jax.ShapeDtypeStruct((1, features, features), jnp.float32),
        in_specs=[smem, smem, pl.BlockSpec(memory_space=pltpu.VMEM)],
        out_specs=pl.BlockSpec(memory_space=pl.ANY),
        scratch_shapes=[
            pltpu.VMEM((features, features), jnp.float32),
            pltpu.SemaphoreType.DMA((features // tile,)),
        ],
        compiler_params=pltpu.CompilerParams(vmem_limit_bytes=32 * 1024 * 1024),
    )(owner, counts, rows)


def solution(mesh):
    return jax.shard_map(
        per_device,
        mesh=mesh,
        in_specs=(P(("expert", "col"), "row"), P(("expert", "col"), None, None, None), P(), P()),
        out_specs=P("expert", "row", "col"),
        check_vma=False,
    )
```

time: 72.6 us -> 19 us (0.26)
  waiting for transfers between devices: 34.7 us -> 0 us
  between operations: 16 us -> 0.01 us
  Pallas kernels: 0 us -> 15.6 us
  blocking collectives: 5.79 us -> 0 us
  other arithmetic: 4.34 us -> 0 us
  starting transfers between devices: 4.21 us -> 0 us
  matrix products: 3.22 us -> 0 us
  local copies, waits for them, and re-layouts: 3.98 us -> 3.21 us
    psum x1 -> x0, waiting for transfers between devices: 30.7 us -> none  [from_root(): return lax.psum(jnp.where(mine, value, jnp.zeros_like(value)), axis)]
    pallas_call x0 -> x2, Pallas kernels: none -> 15.6 us  [the longest x1 13 us: per_device(): pl.pallas_call(functools.partial(exchange, (n_group, n_row, n_col)), out_...]
    all_gather x1 -> x0, blocking collectives: 5.79 us -> none  [panel_moment(): left_rows = lax.all_gather(received, 'col', axis=2, tiled=True)]
    all_to_all x1 -> x0, starting transfers between devices: 4.21 us -> none  [panel_moment(): lax.all_to_all(outgoing, 'expert', split_axis=1, concat_axis=1, tiled=True)]
    all_to_all x1 -> x0, waiting for transfers between devices: 4 us -> none  [panel_moment(): lax.all_to_all(outgoing, 'expert', split_axis=1, concat_axis=1, tiled=True)]
    dot_general x1 -> x0, matrix products: 3.22 us -> none  [panel_moment(): jnp.einsum('kpa,kpb->ab', left_rows, right_rows, preferred_element_type=j...]
    unnamed x2 -> x6, local copies, waits for them, and re-layouts: 0.01 us -> 3.21 us
    gather x4 -> x0, local copies, waits for them, and re-layouts: 3.14 us -> none  [the longest x1 1.25 us: per_device(): dest_slots = jnp.take(slots[0], inverse, axis=1)]
  transfers between devices with their start and end apart: 2 -> 0, of which waited for: 2 -> 0; matrix products, arithmetic and copies ran while one was open for 3% -> 0% of each run, Pallas kernels for 0% -> 0%
where the time goes in v1:
time: 19 us; the launch traced here: 18.8 us
  Pallas kernels  15.6 us (82%)
  local copies, waits for them, and re-layouts  3.21 us (17%)
    pallas_call x1, Pallas kernels, per_device(): pl.pallas_call(functools.partial(exchange, (n_group, n_row, n_col)), out_...  13 us
    unnamed x6, local copies, waits for them, and re-layouts  3.21 us
    pallas_call x1, Pallas kernels, per_device(): pl.pallas_call(functools.partial(multiply, tile), out_shape=jax.ShapeDtyp...  2.59 us

profile of v1, /device:TPU:0, one launch (start us, length us, event | category | flops | bytes accessed | tf_op | source)
XLA Modules:
  0.0 18.8 jit_solution(10801082962139601550)
XLA Ops:
  0.0 0.8 %copy.7.counts_ref = s32[6,2]{1,0:T(8,128)S(1)} copy(s32[6,2]{0,1:T(2,128)} %param.6) | data formatting | bytes 96 | tf_op args[2]
  0.8 0.8 %copy.6.slots_ref = s32[1,6,2,2]{3,2,1,0:T(2,128)S(1)} copy(s32[1,6,2,2]{1,3,2,0:T(2,128)} %param.5) | data formatting | bytes 192 | tf_op args[1]
  1.5 0.0 copy-start
  1.5 1.0 %copy-done = bf16[256,896]{1,0:T(8,128)(2,1)S(1)} copy-done((bf16[256,896]{1,0:T(8,128)(2,1)S(1)}, bf16[256,896]{1,0:T(8,128)(2,1)}, u32[]{:S(2)}) %copy-start) | copy-done | bytes 458776
  2.6 0.0 copy-start.1
  2.6 0.7 %copy-done.1 = s32[2]{0:T(128)S(1)} copy-done((s32[2]{0:T(128)S(1)}, s32[2]{0:T(128)}, u32[]{:S(2)}) %copy-start.1) | copy-done | bytes 32
  3.2 13.0 %shard_map.46.rows_ref = bf16[2,8,16,896]{3,2,1,0:T(8,128)(2,1)S(1)} custom-call(s32[2]{0:T(128)S(1)} %copy-done.1, s32[6,2]{1,0:T(8,128)S(1)} %copy.7.counts_ref, s32[1,6,2,2]{3,2,1,0:T(2,128)S(1)} %copy.6.slots_ref, bf16[256,896]{1,0:T(8,128)(2,1)S(1)} %copy-done), custom_call_target="tpu_custom_call" | custom-call | tf_op jit(solution)/shard_map/pallas_call | solution.py:195
  16.2 2.6 %shard_map.47 = f32[1,896,896]{2,1,0:T(8,128)} custom-call(s32[2]{0:T(128)S(1)} %copy-done.1, s32[6,2]{1,0:T(8,128)S(1)} %copy.7.counts_ref, bf16[2,8,16,896]{3,2,1,0:T(8,128)(2,1)S(1)} %shard_map.46.rows_ref), custom_call_target="tpu_custom_call" | custom-call | tf_op jit(solution)/shard_map/pallas_call | solution.py:213
Async XLA Ops:
  1.5 1.0 %copy-start = (bf16[256,896]{1,0:T(8,128)(2,1)S(1)}, bf16[256,896]{1,0:T(8,128)(2,1)}, u32[]{:S(2)}) copy-start(bf16[256,896]{1,0:T(8,128)(2,1)} %tokens_ref.1) | copy-start | bytes 1376260
  2.6 0.7 %copy-start.1 = (s32[2]{0:T(128)S(1)}, s32[2]{0:T(128)}, u32[]{:S(2)}) copy-start(s32[2]{0:T(128)} %owner_ref.3) | copy-start | bytes 28

commit v2 on v1

--- a/solution.py
+++ b/solution.py
@@ -29,17 +29,26 @@
     return found
 
 
-def exchange(sizes, owner_ref, counts_ref, slots_ref, tokens_ref, buf, tokens, picked, token_sem, own_sem, send_sem, recv_sem):
+def exchange(
+    sizes, tile, owner_hbm, counts_hbm, slots_hbm, tokens_hbm, out_ref,
+    owner_ref, counts_ref, slots_ref, tokens, picked, buf, load_sem, own_sem, send_sem, recv_sem,
+):
     n_group, n_row, n_col = sizes
-    block_tokens, features = tokens_ref.shape
-    panels, experts = counts_ref.shape
-    slot_count = slots_ref.shape[3]
+    block_tokens, features = tokens.shape
+    experts, panels = counts_ref.shape
+    slot_count = slots_ref.shape[2]
     padded = picked.shape[1]
     x, r, c = lax.axis_index("expert"), lax.axis_index("row"), lax.axis_index("col")
     block = x * n_col + c
 
-    load = pltpu.make_async_copy(tokens_ref, tokens, token_sem)
-    load.start()
+    loads = [
+        pltpu.make_async_copy(source, target, load_sem.at[i])
+        for i, (source, target) in enumerate(
+            [(tokens_hbm, tokens), (slots_hbm, slots_ref), (counts_hbm, counts_ref), (owner_hbm, owner_ref)]
+        )
+    ]
+    for load in loads:
+        load.start()
 
     barrier = pltpu.get_barrier_semaphore()
 
@@ -63,7 +72,8 @@
     def _():
         greet(c, 0, False)
 
-    load.wait()
+    for load in loads:
+        load.wait()
     rows_iota = lax.broadcasted_iota(jnp.int32, (padded, block_tokens), 0)
     token_iota = lax.broadcasted_iota(jnp.int32, (padded, block_tokens), 1)
 
@@ -72,9 +82,9 @@
         e = expert_of(owner_ref, group, experts)
         index = jnp.full((padded, block_tokens), -1, jnp.int32)
         for k in range(panels):
-            count = counts_ref[k, e]
+            count = counts_ref[e, k]
             for j in range(slot_count):
-                slot = jnp.where(block * slot_count + j < count, slots_ref[0, k, e, j], jnp.int32(-1))
+                slot = jnp.where(block * slot_count + j < count, slots_ref[0, e, j, k], jnp.int32(-1))
                 index = jnp.where(rows_iota == k * slot_count + j, slot, index)
         onehot = (index == token_iota).astype(jnp.bfloat16)
         picked[group] = jnp.dot(onehot, tokens[...], preferred_element_type=jnp.float32).astype(jnp.bfloat16)
@@ -160,29 +170,17 @@
     def _():
         each(n_group, wait_right)
 
-
-def multiply(tile, owner_ref, counts_ref, rows_ref, out_ref, product, sems):
-    panels, experts = counts_ref.shape
-    features = rows_ref.shape[-1]
-    x, r, c = lax.axis_index("expert"), lax.axis_index("row"), lax.axis_index("col")
     e = expert_of(owner_ref, x, experts)
     total = jnp.int32(0)
     for k in range(panels):
-        total = total + counts_ref[k, e]
+        total = total + counts_ref[e, k]
     scale = 1.0 / jnp.full((1, features), total, jnp.int32).astype(jnp.float32)
-    side = jnp.where(r == c, 0, 1)
-    right = rows_ref[side].reshape(-1, features)
-    copies = []
+    right_rows = buf[jnp.where(r == c, 0, 1)].reshape(-1, features)
     for t in range(features // tile):
         span = pl.ds(t * tile, tile)
-        left = rows_ref[0, :, :, span].reshape(-1, tile)
-        part = lax.dot_general(left, right, (((0,), (0,)), ((), ())), preferred_element_type=jnp.float32)
-        product[span, :] = part * scale
-        copy = pltpu.make_async_copy(product.at[span, :], out_ref.at[0, span, :], sems.at[t])
-        copy.start()
-        copies.append(copy)
-    for copy in copies:
-        copy.wait()
+        left_rows = buf[0, :, :, span].reshape(-1, tile)
+        part = lax.dot_general(left_rows, right_rows, (((0,), (0,)), ((), ())), preferred_element_type=jnp.float32)
+        out_ref[0, span, :] = part * scale
 
 
 def per_device(tokens, slots, counts, owner):
@@ -191,16 +189,22 @@
     panels, slot_count = counts.shape[0], slots.shape[3]
     padded = -(-panels * slot_count // 16) * 16
     blocks = n_group * n_col
-    smem = pl.BlockSpec(memory_space=pltpu.SMEM)
-    rows = pl.pallas_call(
-        functools.partial(exchange, (n_group, n_row, n_col)),
-        out_shape=jax.ShapeDtypeStruct((2, blocks, padded, features), tokens.dtype),
-        in_specs=[smem, smem, smem, pl.BlockSpec(memory_space=pl.ANY)],
+    counts = counts.T
+    slots = jnp.transpose(slots, (0, 2, 3, 1))
+    hbm = pl.BlockSpec(memory_space=pltpu.HBM)
+    return pl.pallas_call(
+        functools.partial(exchange, (n_group, n_row, n_col), 128),
+        out_shape=jax.ShapeDtypeStruct((1, features, features), jnp.float32),
+        in_specs=[hbm, hbm, hbm, hbm],
         out_specs=pl.BlockSpec(memory_space=pltpu.VMEM),
         scratch_shapes=[
+            pltpu.SMEM(owner.shape, jnp.int32),
+            pltpu.SMEM(counts.shape, jnp.int32),
+            pltpu.SMEM(slots.shape, jnp.int32),
             pltpu.VMEM((block_tokens, features), tokens.dtype),
             pltpu.VMEM((n_group, padded, features), tokens.dtype),
-            pltpu.SemaphoreType.DMA,
+            pltpu.VMEM((2, blocks, padded, features), tokens.dtype),
+            pltpu.SemaphoreType.DMA((4,)),
             pltpu.SemaphoreType.DMA,
             pltpu.SemaphoreType.DMA((2, n_group, max(n_row, n_col))),
             pltpu.SemaphoreType.DMA((2, blocks)),
@@ -208,19 +212,7 @@
         compiler_params=pltpu.CompilerParams(
             collective_id=0, has_side_effects=True, vmem_limit_bytes=32 * 1024 * 1024
         ),
-    )(owner, counts, slots, tokens)
-    tile = 128
-    return pl.pallas_call(
-        functools.partial(multiply, tile),
-        out_shape=jax.ShapeDtypeStruct((1, features, features), jnp.float32),
-        in_specs=[smem, smem, pl.BlockSpec(memory_space=pltpu.VMEM)],
-        out_specs=pl.BlockSpec(memory_space=pl.ANY),
-        scratch_shapes=[
-            pltpu.VMEM((features, features), jnp.float32),
-            pltpu.SemaphoreType.DMA((features // tile,)),
-        ],
-        compiler_params=pltpu.CompilerParams(vmem_limit_bytes=32 * 1024 * 1024),
-    )(owner, counts, rows)
+    )(*[pltpu.with_memory_space_constraint(a, pltpu.HBM) for a in (owner, counts, slots, tokens)])
 
 
 def solution(mesh):

time: 19 us -> 14.3 us (0.75)
  Pallas kernels: 15.6 us -> 12.4 us
  local copies, waits for them, and re-layouts: 3.21 us -> 1.69 us
    pallas_call x2 -> x1, Pallas kernels: 15.6 us -> 12.4 us  [per_device(): pl.pallas_call(functools.partial(exchange, (n_group, n_row, n_col), 128),...]
    unnamed x6 -> x1, local copies, waits for them, and re-layouts: 3.21 us -> 1.69 us
where the time goes in v2:
time: 14.3 us; the launch traced here: 14.1 us
  Pallas kernels  12.4 us (87%)
  local copies, waits for them, and re-layouts  1.69 us (12%)
    pallas_call x1, Pallas kernels, per_device(): pl.pallas_call(functools.partial(exchange, (n_group, n_row, n_col), 128),...  12.4 us
    unnamed x1, local copies, waits for them, and re-layouts  1.69 us

profile of v2, /device:TPU:0, one launch (start us, length us, event | category | flops | bytes accessed | tf_op | source)
XLA Modules:
  0.0 14.1 jit_solution(11931329511662703755)
XLA Ops:
  0.0 12.4 %shard_map.46 = f32[1,896,896]{2,1,0:T(8,128)S(1)} custom-call(s32[2]{0:T(128)} %owner_hbm.1, s32[2,6]{1,0:T(2,128)} %bitcast.3, s32[1,2,2,6]{3,2,1,0:T(2,128)} %bitcast.2, bf16[256,896]{1,0:T(8,128)(2,1)} %tokens_hbm.1), custom_call_target="tpu_custom_call" | custom-call | tf_op jit(solution)/shard_map/pallas_call | solution.py:195
  12.4 1.7 %copy.6 = f32[1,896,896]{2,1,0:T(8,128)} copy(f32[1,896,896]{2,1,0:T(8,128)S(1)} %shard_map.46) | data formatting | bytes 6422528

commit v3 on v2

v3 whole, which is shorter than its diff:
```python
import functools

import jax
import jax.numpy as jnp
from jax import lax
from jax.experimental import pallas as pl
from jax.experimental.pallas import tpu as pltpu
from jax.sharding import PartitionSpec as P

MESH = pl.DeviceIdType.MESH


def each(count, body):
    if count <= 4:
        for i in range(count):
            body(i)
    else:
        pl.loop(0, count)(body)


def unless_self(dg, dc, act):
    if dc > 0 or (isinstance(dg, int) and dg > 0):
        act()
    elif not isinstance(dg, int):
        pl.when(dg > 0)(act)


def wrap(index, count):
    return lax.rem(index + count, count)


def expert_of(owner_ref, group, expert_count):
    found = jnp.int32(0)
    for e in range(expert_count):
        found = jnp.where(owner_ref[e] == group, jnp.int32(e), found)
    return found


def exchange(
    sizes, tile, owner_hbm, counts_hbm, slots_hbm, tokens_hbm, out_ref,
    owner_ref, counts_ref, slots_ref, tokens, picked, packed, landed, buf,
    load_sem, own_sem, line_send, line_recv, send_sem, recv_sem,
):
    n_group, n_row, n_col = sizes
    block_tokens, features = tokens.shape
    experts, panels = counts_ref.shape
    slot_count = slots_ref.shape[2]
    per_group = panels * slot_count
    tiles = picked.shape[1]
    x, r, c = lax.axis_index("expert"), lax.axis_index("row"), lax.axis_index("col")
    block = x * n_col + c

    loads = [
        pltpu.make_async_copy(source, target, load_sem.at[i])
        for i, (source, target) in enumerate(
            [(tokens_hbm, tokens), (slots_hbm, slots_ref), (counts_hbm, counts_ref), (owner_hbm, owner_ref)]
        )
    ]
    for load in loads:
        load.start()

    barrier = pltpu.get_barrier_semaphore()

    def greet(dg):
        for dc in range(n_col):
            def signal(dc=dc):
                pl.semaphore_signal(
                    barrier, inc=1, device_id=(wrap(x + dg, n_group), r, wrap(c + dc, n_col)), device_id_type=MESH
                )
            unless_self(dg, dc, signal)

    for dr in range(1, n_row):
        pl.semaphore_signal(barrier, inc=1, device_id=(x, wrap(r + dr, n_row), c), device_id_type=MESH)
    each(n_group, greet)

    for load in loads:
        load.wait()
    rows_iota = lax.broadcasted_iota(jnp.int32, (tiles * 8, block_tokens), 0)
    token_iota = lax.broadcasted_iota(jnp.int32, (tiles * 8, block_tokens), 1)
    packed[...] = jnp.zeros_like(packed)

    def first_tile(group):
        return (group * per_group) // 8

    def pick(group):
        e = expert_of(owner_ref, group, experts)
        skipped = group * per_group - first_tile(group) * 8
        index = jnp.full((tiles * 8, block_tokens), -1, jnp.int32)
        for k in range(panels):
            count = counts_ref[e, k]
            for j in range(slot_count):
                slot = jnp.where(block * slot_count + j < count, slots_ref[0, e, j, k], jnp.int32(-1))
                index = jnp.where(rows_iota == k * slot_count + j + skipped, slot, index)
        onehot = (index == token_iota).astype(jnp.bfloat16)
        rows = jnp.dot(onehot, tokens[...], preferred_element_type=jnp.float32)
        rows = rows.reshape(tiles, 8, features).astype(jnp.bfloat16)
        picked[group] = rows
        window = pl.ds(first_tile(group), tiles)
        packed[window] = packed[window] + rows

    each(n_group, pick)
    pl.semaphore_wait(barrier, n_row - 1 + n_group * n_col - 1)

    def line_copy(dr):
        return pltpu.make_async_remote_copy(
            src_ref=packed,
            dst_ref=landed.at[dr - 1],
            send_sem=line_send.at[dr - 1],
            recv_sem=line_recv.at[dr - 1],
            device_id=(x, wrap(r + dr, n_row), c),
            device_id_type=MESH,
        )

    def left_copy(dg, dc):
        group = wrap(x + dg, n_group)
        return pltpu.make_async_remote_copy(
            src_ref=picked.at[group],
            dst_ref=buf.at[0, block],
            send_sem=send_sem.at[0, dg, dc],
            recv_sem=recv_sem.at[0, block],
            device_id=(group, r, wrap(c + dc, n_col)),
            device_id_type=MESH,
        )

    def window_of(dr, group):
        return landed.at[dr - 1, pl.ds(first_tile(group), tiles)]

    def right_copy(dr, dg):
        group = wrap(x + dg, n_group)
        return pltpu.make_async_remote_copy(
            src_ref=window_of(dr, group),
            dst_ref=buf.at[1, block],
            send_sem=send_sem.at[1, dg, dr],
            recv_sem=recv_sem.at[1, block],
            device_id=(group, r, wrap(r - dr, n_row)),
            device_id_type=MESH,
        )

    def own_right(dr):
        return pltpu.make_async_copy(window_of(dr, x), buf.at[1, block], own_sem.at[1])

    for dr in range(1, n_row):
        line_copy(dr).start()
    own_left = pltpu.make_async_copy(picked.at[x], buf.at[0, block], own_sem.at[0])
    own_left.start()

    def lefts(act):
        def body(dg):
            for dc in range(n_col):
                unless_self(dg, dc, lambda dc=dc: act(left_copy(dg, dc)))
        each(n_group, body)

    lefts(lambda copy: copy.start())

    def rights(dr, act, act_own):
        here = c == wrap(r - dr, n_row)
        def body(dg):
            if isinstance(dg, int) and dg > 0:
                act(right_copy(dr, dg))
            else:
                pl.when(jnp.logical_or(jnp.logical_not(here), dg != 0))(lambda: act(right_copy(dr, dg)))
        each(n_group, body)
        if act_own is not None:
            pl.when(here)(lambda: act_own(own_right(dr)))

    for dr in range(1, n_row):
        line_copy(dr).wait_recv()
        rights(dr, lambda copy: copy.start(), lambda copy: copy.start())

    def arrived(side, b):
        pltpu.make_async_remote_copy(
            src_ref=picked.at[0],
            dst_ref=buf.at[side, b],
            send_sem=send_sem.at[0, 0, 0],
            recv_sem=recv_sem.at[side, b],
            device_id=(x, r, c),
            device_id_type=MESH,
        ).wait_recv()

    def wait_side(side):
        def body(dg):
            for dc in range(n_col):
                b = wrap(x + dg, n_group) * n_col + wrap(c + dc, n_col)
                unless_self(dg, dc, lambda b=b: arrived(side, b))
        each(n_group, body)

    e = expert_of(owner_ref, x, experts)
    total = jnp.int32(0)
    for k in range(panels):
        total = total + counts_ref[e, k]
    scale = 1.0 / jnp.full((1, features), total, jnp.int32).astype(jnp.float32)

    own_left.wait()
    wait_side(0)

    @pl.when(r != c)
    def _():
        wait_side(1)
        own_right(1).wait()

    right_rows = buf[jnp.where(r == c, 0, 1)].reshape(-1, features)
    for t in range(features // tile):
        span = pl.ds(t * tile, tile)
        left_rows = buf[0, :, :, :, span].reshape(-1, tile)
        part = lax.dot_general(left_rows, right_rows, (((0,), (0,)), ((), ())), preferred_element_type=jnp.float32)
        out_ref[0, span, :] = part * scale

    for dr in range(1, n_row):
        line_copy(dr).wait_send()
        rights(dr, lambda copy: copy.wait_send(), None)
    lefts(lambda copy: copy.wait_send())


def per_device(tokens, slots, counts, owner):
    n_group, n_row, n_col = lax.axis_size("expert"), lax.axis_size("row"), lax.axis_size("col")
    block_tokens, features = tokens.shape
    panels, slot_count = counts.shape[0], slots.shape[3]
    per_group = panels * slot_count
    blocks = n_group * n_col
    starts = [g * per_group for g in range(n_group)]
    tiles = max((g + per_group + 7) // 8 - g // 8 for g in starts)
    packed_tiles = starts[-1] // 8 + tiles
    counts = counts.T
    slots = jnp.transpose(slots, (0, 2, 3, 1))
    hbm = pl.BlockSpec(memory_space=pltpu.HBM)
    return pl.pallas_call(
        functools.partial(exchange, (n_group, n_row, n_col), 128),
        out_shape=jax.ShapeDtypeStruct((1, features, features), jnp.float32),
        in_specs=[hbm, hbm, hbm, hbm],
        out_specs=pl.BlockSpec(memory_space=pltpu.VMEM),
        scratch_shapes=[
            pltpu.SMEM(owner.shape, jnp.int32),
            pltpu.SMEM(counts.shape, jnp.int32),
            pltpu.SMEM(slots.shape, jnp.int32),
            pltpu.VMEM((block_tokens, features), tokens.dtype),
            pltpu.VMEM((n_group, tiles, 8, features), tokens.dtype),
            pltpu.VMEM((packed_tiles, 8, features), tokens.dtype),
            pltpu.VMEM((n_row - 1, packed_tiles, 8, features), tokens.dtype),
            pltpu.VMEM((2, blocks, tiles, 8, features), tokens.dtype),
            pltpu.SemaphoreType.DMA((4,)),
            pltpu.SemaphoreType.DMA((2,)),
            pltpu.SemaphoreType.DMA((n_row - 1,)),
            pltpu.SemaphoreType.DMA((n_row - 1,)),
            pltpu.SemaphoreType.DMA((2, n_group, max(n_row, n_col))),
            pltpu.SemaphoreType.DMA((2, blocks)),
        ],
        compiler_params=pltpu.CompilerParams(
            collective_id=0, has_side_effects=True, vmem_limit_bytes=32 * 1024 * 1024
        ),
    )(*[pltpu.with_memory_space_constraint(a, pltpu.HBM) for a in (owner, counts, slots, tokens)])


def solution(mesh):
    return jax.shard_map(
        per_device,
        mesh=mesh,
        in_specs=(P(("expert", "col"), "row"), P(("expert", "col"), None, None, None), P(), P()),
        out_specs=P("expert", "row", "col"),
        check_vma=False,
    )
```

time: 14.3 us -> 15.9 us (1.11)
  the two profiles are of different devices: /device:TPU:0 before, /device:TPU:1 now
where the time goes in v3:
time: 15.9 us; the launch traced here: 15.8 us
  Pallas kernels  14.1 us (89%)
  local copies, waits for them, and re-layouts  1.69 us (11%)
    pallas_call x1, Pallas kernels, per_device(): pl.pallas_call(functools.partial(exchange, (n_group, n_row, n_col), 128),...  14.1 us
    unnamed x1, local copies, waits for them, and re-layouts  1.69 us

profile of v3, /device:TPU:1, one launch (start us, length us, event | category | flops | bytes accessed | tf_op | source)
XLA Modules:
  0.0 15.8 jit_solution(8294591223816685547)
XLA Ops:
  0.0 14.1 %shard_map.46 = f32[1,896,896]{2,1,0:T(8,128)S(1)} custom-call(s32[2]{0:T(128)} %owner_hbm.1, s32[2,6]{1,0:T(2,128)} %bitcast.3, s32[1,2,2,6]{3,2,1,0:T(2,128)} %bitcast.2, bf16[256,896]{1,0:T(8,128)(2,1)} %tokens_hbm.1), custom_call_target="tpu_custom_call" | custom-call | tf_op jit(solution)/shard_map/pallas_call | solution.py:226
  14.1 1.7 %copy.6 = f32[1,896,896]{2,1,0:T(8,128)} copy(f32[1,896,896]{2,1,0:T(8,128)S(1)} %shard_map.46) | data formatting | bytes 6422528

commit v4 on v2

v4 whole, which is shorter than its diff:
```python
import functools

import jax
import jax.numpy as jnp
from jax import lax
from jax.experimental import pallas as pl
from jax.experimental.pallas import tpu as pltpu
from jax.sharding import PartitionSpec as P

MESH = pl.DeviceIdType.MESH


def each(count, body):
    if count <= 4:
        for i in range(count):
            body(i)
    else:
        pl.loop(0, count)(body)


def wrap(index, count):
    return lax.rem(index + count, count)


def expert_of(owner_ref, group, expert_count):
    found = jnp.int32(0)
    for e in range(expert_count):
        found = jnp.where(owner_ref[e] == group, jnp.int32(e), found)
    return found


def exchange(
    sizes, tile, owner_hbm, counts_hbm, slots_hbm, tokens_hbm, out_ref,
    owner_ref, counts_ref, slots_ref, tokens, picked, landed, merged, buf,
    load_sem, own_sem, pair_send, pair_recv, send_sem, recv_sem,
):
    n_group, n_row, n_col = sizes
    block_tokens, features = tokens.shape
    experts, panels = counts_ref.shape
    slot_count = slots_ref.shape[2]
    per_group = panels * slot_count
    _, n_handled, tiles = picked.shape[:3]
    n_pair = n_col // 2
    x, r, c = lax.axis_index("expert"), lax.axis_index("row"), lax.axis_index("col")
    block = x * n_col + c
    parity = c % 2
    partner = c + 1 - 2 * parity

    loads = [
        pltpu.make_async_copy(source, target, load_sem.at[i])
        for i, (source, target) in enumerate(
            [(tokens_hbm, tokens), (slots_hbm, slots_ref), (counts_hbm, counts_ref), (owner_hbm, owner_ref)]
        )
    ]
    for load in loads:
        load.start()

    barrier = pltpu.get_barrier_semaphore()

    def signal(device):
        pl.semaphore_signal(barrier, inc=1, device_id=device, device_id_type=MESH)

    def sender_column(pair):
        return 2 * pair + x % 2

    def greet(row, check):
        def body(dg):
            for pair in range(n_pair):
                device = (wrap(x + dg, n_group), row, sender_column(pair))
                if check:
                    pl.when(jnp.logical_or(device[0] != x, device[2] != c))(lambda device=device: signal(device))
                else:
                    signal(device)
        each(n_group, body)

    signal((x, r, partner))
    greet(r, True)

    @pl.when(r != c)
    def _():
        greet(c, False)

    for load in loads:
        load.wait()
    rows_iota = lax.broadcasted_iota(jnp.int32, (tiles * 8, block_tokens), 0)
    token_iota = lax.broadcasted_iota(jnp.int32, (tiles * 8, block_tokens), 1)

    def first_tile(side):
        return side * (per_group // 8)

    skipped = parity * (per_group % 8)

    def onehot(group):
        e = expert_of(owner_ref, group, experts)
        index = jnp.full((tiles * 8, block_tokens), -1, jnp.int32)
        for k in range(panels):
            count = counts_ref[e, k]
            for j in range(slot_count):
                slot = jnp.where(block * slot_count + j < count, slots_ref[0, e, j, k], jnp.int32(-1))
                index = jnp.where(rows_iota == k * slot_count + j + skipped, slot, index)
        return index == token_iota

    def pick(i):
        chosen = jnp.concatenate([onehot(2 * i), onehot(2 * i + 1)], axis=0).astype(jnp.bfloat16)
        rows = jnp.dot(chosen, tokens[...], preferred_element_type=jnp.float32)
        rows = rows.reshape(2, tiles, 8, features).astype(jnp.bfloat16)
        picked[0, i] = rows[0]
        picked[1, i] = rows[1]

    each(n_handled, pick)

    sends = 1 + n_handled * (n_col + n_row - 1)
    own = x % 2 == parity

    @pl.when(own)
    def _():
        pl.semaphore_wait(barrier, sends - 1)

    @pl.when(jnp.logical_not(own))
    def _():
        pl.semaphore_wait(barrier, sends)

    pair_copy = pltpu.make_async_remote_copy(
        src_ref=picked.at[1 - parity],
        dst_ref=landed,
        send_sem=pair_send,
        recv_sem=pair_recv,
        device_id=(x, r, partner),
        device_id_type=MESH,
    )
    pair_copy.start()
    merged[...] = jnp.zeros_like(merged)
    merged[:, pl.ds(first_tile(parity), tiles)] = picked[parity]
    pair_copy.wait_recv()
    window = pl.ds(first_tile(1 - parity), tiles)
    merged[:, window] = merged[:, window] + landed[...]

    my_slot = x * n_pair + c // 2

    def handled(di):
        return wrap(x // 2 + di, n_handled)

    def right_copy(di, dr):
        return pltpu.make_async_remote_copy(
            src_ref=merged.at[handled(di)],
            dst_ref=buf.at[1, my_slot],
            send_sem=send_sem.at[1, di, dr],
            recv_sem=recv_sem.at[1, my_slot],
            device_id=(2 * handled(di) + parity, wrap(r + dr, n_row), r),
            device_id_type=MESH,
        )

    def left_copy(di, dc):
        return pltpu.make_async_remote_copy(
            src_ref=merged.at[handled(di)],
            dst_ref=buf.at[0, my_slot],
            send_sem=send_sem.at[0, di, dc],
            recv_sem=recv_sem.at[0, my_slot],
            device_id=(2 * handled(di) + parity, r, wrap(c + dc, n_col)),
            device_id_type=MESH,
        )

    def rights(act):
        def body(di):
            for dr in range(1, n_row):
                act(right_copy(di, dr))
        each(n_handled, body)

    def lefts(act):
        def body(di):
            for dc in range(1, n_col):
                act(left_copy(di, dc))
            pl.when(2 * handled(di) + parity != x)(lambda: act(left_copy(di, 0)))
        each(n_handled, body)

    own_copy = pltpu.make_async_copy(merged.at[x // 2], buf.at[0, my_slot], own_sem)
    rights(lambda copy: copy.start())
    lefts(lambda copy: copy.start())
    pl.when(own)(own_copy.start)

    def arrived(side, slot):
        pltpu.make_async_remote_copy(
            src_ref=merged.at[0],
            dst_ref=buf.at[side, slot],
            send_sem=pair_send,
            recv_sem=recv_sem.at[side, slot],
            device_id=(x, r, partner),
            device_id_type=MESH,
        ).wait_recv()

    def wait_left(dg):
        group = wrap(x + dg, n_group)
        for pair in range(n_pair):
            sender = sender_column(pair)
            pl.when(jnp.logical_or(group != x, sender != c))(lambda pair=pair: arrived(0, group * n_pair + pair))

    def wait_right(dg):
        for pair in range(n_pair):
            arrived(1, wrap(x + dg, n_group) * n_pair + pair)

    e = expert_of(owner_ref, x, experts)
    total = jnp.int32(0)
    for k in range(panels):
        total = total + counts_ref[e, k]
    scale = 1.0 / jnp.full((1, features), total, jnp.int32).astype(jnp.float32)

    pl.when(own)(own_copy.wait)
    each(n_group, wait_left)

    @pl.when(r != c)
    def _():
        each(n_group, wait_right)

    right_rows = buf[jnp.where(r == c, 0, 1)].reshape(-1, features)
    for t in range(features // tile):
        span = pl.ds(t * tile, tile)
        left_rows = buf[0, :, :, :, span].reshape(-1, tile)
        part = lax.dot_general(left_rows, right_rows, (((0,), (0,)), ((), ())), preferred_element_type=jnp.float32)
        out_ref[0, span, :] = part * scale

    pair_copy.wait_send()
    rights(lambda copy: copy.wait_send())
    lefts(lambda copy: copy.wait_send())


def per_device(tokens, slots, counts, owner):
    n_group, n_row, n_col = lax.axis_size("expert"), lax.axis_size("row"), lax.axis_size("col")
    block_tokens, features = tokens.shape
    panels, slot_count = counts.shape[0], slots.shape[3]
    per_group = panels * slot_count
    n_handled, slots_in = n_group // 2, n_group * n_col // 2
    tiles = (per_group % 8 + per_group + 7) // 8
    merged_tiles = per_group // 8 + tiles
    tile = features if slots_in * merged_tiles * 8 <= 256 else 128
    counts = counts.T
    slots = jnp.transpose(slots, (0, 2, 3, 1))
    hbm = pl.BlockSpec(memory_space=pltpu.HBM)
    return pl.pallas_call(
        functools.partial(exchange, (n_group, n_row, n_col), tile),
        out_shape=jax.ShapeDtypeStruct((1, features, features), jnp.float32),
        in_specs=[hbm, hbm, hbm, hbm],
        out_specs=pl.BlockSpec(memory_space=pltpu.VMEM),
        scratch_shapes=[
            pltpu.SMEM(owner.shape, jnp.int32),
            pltpu.SMEM(counts.shape, jnp.int32),
            pltpu.SMEM(slots.shape, jnp.int32),
            pltpu.VMEM((block_tokens, features), tokens.dtype),
            pltpu.VMEM((2, n_handled, tiles, 8, features), tokens.dtype),
            pltpu.VMEM((n_handled, tiles, 8, features), tokens.dtype),
            pltpu.VMEM((n_handled, merged_tiles, 8, features), tokens.dtype),
            pltpu.VMEM((2, slots_in, merged_tiles, 8, features), tokens.dtype),
            pltpu.SemaphoreType.DMA((4,)),
            pltpu.SemaphoreType.DMA,
            pltpu.SemaphoreType.DMA,
            pltpu.SemaphoreType.DMA,
            pltpu.SemaphoreType.DMA((2, n_handled, max(n_row, n_col))),
            pltpu.SemaphoreType.DMA((2, slots_in)),
        ],
        compiler_params=pltpu.CompilerParams(
            collective_id=0, has_side_effects=True, vmem_limit_bytes=32 * 1024 * 1024
        ),
    )(*[pltpu.with_memory_space_constraint(a, pltpu.HBM) for a in (owner, counts, slots, tokens)])


def solution(mesh):
    return jax.shard_map(
        per_device,
        mesh=mesh,
        in_specs=(P(("expert", "col"), "row"), P(("expert", "col"), None, None, None), P(), P()),
        out_specs=P("expert", "row", "col"),
        check_vma=False,
    )
```

time: 14.3 us -> 14.3 us (level)
  no operation moved by 1% of the time
where the time goes in v4:
time: 14.3 us; the launch traced here: 14.2 us
  Pallas kernels  12.5 us (87%)
  local copies, waits for them, and re-layouts  1.69 us (12%)
    pallas_call x1, Pallas kernels, per_device(): pl.pallas_call(functools.partial(exchange, (n_group, n_row, n_col), tile)...  12.5 us
    unnamed x1, local copies, waits for them, and re-layouts  1.69 us

profile of v4, /device:TPU:0, one launch (start us, length us, event | category | flops | bytes accessed | tf_op | source)
XLA Modules:
  0.0 14.2 jit_solution(3771819088388417118)
XLA Ops:
  0.0 12.5 %shard_map.46 = f32[1,896,896]{2,1,0:T(8,128)S(1)} custom-call(s32[2]{0:T(128)} %owner_hbm.1, s32[2,6]{1,0:T(2,128)} %bitcast.3, s32[1,2,2,6]{3,2,1,0:T(2,128)} %bitcast.2, bf16[256,896]{1,0:T(8,128)(2,1)} %tokens_hbm.1), custom_call_target="tpu_custom_call" | custom-call | tf_op jit(solution)/shard_map/pallas_call | solution.py:238
  12.5 1.7 %copy.6 = f32[1,896,896]{2,1,0:T(8,128)} copy(f32[1,896,896]{2,1,0:T(8,128)S(1)} %shard_map.46) | data formatting | bytes 6422528

commit v5 on v4

--- a/solution.py
+++ b/solution.py
@@ -31,8 +31,8 @@
 
 def exchange(
     sizes, tile, owner_hbm, counts_hbm, slots_hbm, tokens_hbm, out_ref,
-    owner_ref, counts_ref, slots_ref, tokens, picked, landed, merged, buf,
-    load_sem, own_sem, pair_send, pair_recv, send_sem, recv_sem,
+    owner_ref, counts_ref, slots_ref, tokens, picked, landed, merged, relay, buf,
+    load_sem, own_sem, pair_send, pair_recv, relay_send, relay_recv, send_sem, recv_sem,
 ):
     n_group, n_row, n_col = sizes
     block_tokens, features = tokens.shape
@@ -63,24 +63,27 @@
     def sender_column(pair):
         return 2 * pair + x % 2
 
-    def greet(row, check):
-        def body(dg):
-            for pair in range(n_pair):
-                device = (wrap(x + dg, n_group), row, sender_column(pair))
-                if check:
-                    pl.when(jnp.logical_or(device[0] != x, device[2] != c))(lambda device=device: signal(device))
-                else:
-                    signal(device)
-        each(n_group, body)
+    own = x % 2 == parity
+
+    def greet_lefts(dg):
+        for pair in range(n_pair):
+            device = (wrap(x + dg, n_group), r, sender_column(pair))
+            pl.when(jnp.logical_or(device[0] != x, device[2] != c))(lambda device=device: signal(device))
+
+    def relays(dr):
+        return jnp.logical_and(own, wrap(r - dr, n_row) // 2 != c // 2)
+
+    def greet_rights(dg):
+        group = wrap(x + dg, n_group)
+        pl.when(r != c)(lambda: signal((group, c, sender_column(c // 2))))
+        for dr in range(1, n_row):
+            pl.when(relays(dr))(lambda dr=dr: signal((group, wrap(r - dr, n_row), c)))
 
     signal((x, r, partner))
-    greet(r, True)
-
-    @pl.when(r != c)
-    def _():
-        greet(c, False)
-
-    for load in loads:
+    each(n_group, greet_rights)
+    each(n_group, greet_lefts)
+
+    for load in loads[1:]:
         load.wait()
     rows_iota = lax.broadcasted_iota(jnp.int32, (tiles * 8, block_tokens), 0)
     token_iota = lax.broadcasted_iota(jnp.int32, (tiles * 8, block_tokens), 1)
@@ -100,17 +103,24 @@
                 index = jnp.where(rows_iota == k * slot_count + j + skipped, slot, index)
         return index == token_iota
 
-    def pick(i):
-        chosen = jnp.concatenate([onehot(2 * i), onehot(2 * i + 1)], axis=0).astype(jnp.bfloat16)
+    def choose(i):
+        return jnp.concatenate([onehot(2 * i), onehot(2 * i + 1)], axis=0).astype(jnp.bfloat16)
+
+    def pick(i, chosen):
         rows = jnp.dot(chosen, tokens[...], preferred_element_type=jnp.float32)
         rows = rows.reshape(2, tiles, 8, features).astype(jnp.bfloat16)
         picked[0, i] = rows[0]
         picked[1, i] = rows[1]
 
-    each(n_handled, pick)
+    if n_handled == 1:
+        chosen = choose(0)
+        loads[0].wait()
+        pick(0, chosen)
+    else:
+        loads[0].wait()
+        each(n_handled, lambda i: pick(i, choose(i)))
 
     sends = 1 + n_handled * (n_col + n_row - 1)
-    own = x % 2 == parity
 
     @pl.when(own)
     def _():
@@ -140,15 +150,42 @@
     def handled(di):
         return wrap(x // 2 + di, n_handled)
 
-    def right_copy(di, dr):
+    relayed = c // 2 != r // 2
+
+    def right_copy(di, dr, by_relay):
         return pltpu.make_async_remote_copy(
             src_ref=merged.at[handled(di)],
-            dst_ref=buf.at[1, my_slot],
+            dst_ref=relay.at[x, dr - 1] if by_relay else buf.at[1, my_slot],
             send_sem=send_sem.at[1, di, dr],
-            recv_sem=recv_sem.at[1, my_slot],
-            device_id=(2 * handled(di) + parity, wrap(r + dr, n_row), r),
+            recv_sem=relay_recv.at[x, dr - 1] if by_relay else recv_sem.at[1, my_slot],
+            device_id=(2 * handled(di) + parity, wrap(r + dr, n_row), c if by_relay else r),
             device_id_type=MESH,
         )
+
+    def forward_copy(dr, source):
+        return pltpu.make_async_remote_copy(
+            src_ref=relay.at[source, dr - 1],
+            dst_ref=buf.at[1, source * n_pair + c // 2],
+            send_sem=relay_send.at[source, dr - 1],
+            recv_sem=recv_sem.at[1, source * n_pair + c // 2],
+            device_id=(x, r, wrap(r - dr, n_row)),
+            device_id_type=MESH,
+        )
+
+    def forwards(act):
+        for dr in range(1, n_row):
+            pl.when(relays(dr))(lambda dr=dr: each(n_group, lambda dg: act(dr, wrap(x + dg, n_group))))
+
+    def forward(dr, source):
+        pltpu.make_async_remote_copy(
+            src_ref=merged.at[0],
+            dst_ref=relay.at[source, dr - 1],
+            send_sem=pair_send,
+            recv_sem=relay_recv.at[source, dr - 1],
+            device_id=(x, r, partner),
+            device_id_type=MESH,
+        ).wait_recv()
+        forward_copy(dr, source).start()
 
     def left_copy(di, dc):
         return pltpu.make_async_remote_copy(
@@ -161,10 +198,13 @@
         )
 
     def rights(act):
-        def body(di):
-            for dr in range(1, n_row):
-                act(right_copy(di, dr))
-        each(n_handled, body)
+        def some(by_relay):
+            def body(di):
+                for dr in range(1, n_row):
+                    act(right_copy(di, dr, by_relay))
+            each(n_handled, body)
+        pl.when(relayed)(lambda: some(True))
+        pl.when(jnp.logical_not(relayed))(lambda: some(False))
 
     def lefts(act):
         def body(di):
@@ -177,6 +217,7 @@
     rights(lambda copy: copy.start())
     lefts(lambda copy: copy.start())
     pl.when(own)(own_copy.start)
+    forwards(forward)
 
     def arrived(side, slot):
         pltpu.make_async_remote_copy(
@@ -221,6 +262,7 @@
     pair_copy.wait_send()
     rights(lambda copy: copy.wait_send())
     lefts(lambda copy: copy.wait_send())
+    forwards(lambda dr, source: forward_copy(dr, source).wait_send())
 
 
 def per_device(tokens, slots, counts, owner):
@@ -248,11 +290,14 @@
             pltpu.VMEM((2, n_handled, tiles, 8, features), tokens.dtype),
             pltpu.VMEM((n_handled, tiles, 8, features), tokens.dtype),
             pltpu.VMEM((n_handled, merged_tiles, 8, features), tokens.dtype),
+            pltpu.VMEM((n_group, n_row - 1, merged_tiles, 8, features), tokens.dtype),
             pltpu.VMEM((2, slots_in, merged_tiles, 8, features), tokens.dtype),
             pltpu.SemaphoreType.DMA((4,)),
             pltpu.SemaphoreType.DMA,
             pltpu.SemaphoreType.DMA,
             pltpu.SemaphoreType.DMA,
+            pltpu.SemaphoreType.DMA((n_group, n_row - 1)),
+            pltpu.SemaphoreType.DMA((n_group, n_row - 1)),
             pltpu.SemaphoreType.DMA((2, n_handled, max(n_row, n_col))),
             pltpu.SemaphoreType.DMA((2, slots_in)),
         ],

time: 14.3 us -> 16.4 us (1.15)
  the two profiles are of different devices: /device:TPU:0 before, /device:TPU:24 now
where the time goes in v5:
time: 16.4 us; the launch traced here: 16.2 us
  Pallas kernels  14.5 us (88%)
  local copies, waits for them, and re-layouts  1.69 us (10%)
    pallas_call x1, Pallas kernels, per_device(): pl.pallas_call(functools.partial(exchange, (n_group, n_row, n_col), tile)...  14.5 us
    unnamed x1, local copies, waits for them, and re-layouts  1.69 us

profile of v5, /device:TPU:24, one launch (start us, length us, event | category | flops | bytes accessed | tf_op | source)
XLA Modules:
  0.0 16.2 jit_solution(9480409617718053333)
XLA Ops:
  0.0 14.5 %shard_map.46 = f32[1,896,896]{2,1,0:T(8,128)S(1)} custom-call(s32[2]{0:T(128)} %owner_hbm.1, s32[2,6]{1,0:T(2,128)} %bitcast.3, s32[1,2,2,6]{3,2,1,0:T(2,128)} %bitcast.2, bf16[256,896]{1,0:T(8,128)(2,1)} %tokens_hbm.1), custom_call_target="tpu_custom_call" | custom-call | tf_op jit(solution)/shard_map/pallas_call | solution.py:280
  14.5 1.7 %copy.6 = f32[1,896,896]{2,1,0:T(8,128)} copy(f32[1,896,896]{2,1,0:T(8,128)S(1)} %shard_map.46) | data formatting | bytes 6422528
